TPU v7x, 32 devices: a whole 2x2x4 slice. The times are simulated.
32 devices in a mesh: groups: 2 (over y), fsdp: 8 (over z, x), dp: 1, sub: 2 (over core).
Axes of the slice: x: 2, y: 2, z: 4, core: 2. Of those that a mesh axis runs over, the one named last changes fastest.
Arguments:
- features: bfloat16 [16, 768, 1280], P(('groups', 'fsdp', 'dp'), 'sub'), parts along dimension 0, may hold values from -6 to 6
- golden: bfloat16 [4, 768, 1280], P(('groups', 'dp'), 'sub'), parts along dimension 0, may hold values from -6 to 6
- die_wafer: int32 [16], P(('groups', 'fsdp', 'dp')), parts along dimension 0, may hold values from 0 to 1
- norm_gain: float32 [1280], replicated, may hold values from 0.1 to 1.9
- proj_weight: bfloat16 [1280, 2560], P('fsdp'), may hold values from -0.15625 to 0.15625
- out_weight: bfloat16 [2560, 1280], P('fsdp'), may hold values from -0.125 to 0.125
- zero_weight: bfloat16 [1280, 1280], P(None, 'fsdp'), may hold values from -0.15625 to 0.15625
Outputs:
- block_out: bfloat16 [16, 768, 1280], P(('groups', 'fsdp', 'dp'), 'sub'), parts along dimension 0
There are 2 independent parts, one for each index of `groups`. A program takes and returns all parts, laid end to end along the dimension named above; an argument that names none is the same for every part. Nothing has to cross between parts.
All inputs are finite; a program needn't handle non-finite values.
Results may differ from a plain program's by a relative error of at most 0.005.
Values may be sent and summed in bfloat16 or wider, within the bound.
A program may use at most 128 MiB of HBM per device.

v0:
```python
import jax
import jax.numpy as jnp
from jax import lax
from jax.sharding import PartitionSpec as P


def body(features, golden, die_wafer, norm_gain, proj_weight, out_weight, zero_weight):
    wafer_one = die_wafer[0]
    columns = jnp.einsum(
        "wpc,cd->wpd", golden, zero_weight, preferred_element_type=jnp.float32
    ).astype(jnp.bfloat16)
    gathered = lax.all_gather(columns, "fsdp", axis=2, tiled=True)
    residual = lax.dynamic_index_in_dim(gathered, wafer_one, 0, keepdims=False)
    mixed = features[0].astype(jnp.float32) + residual.astype(jnp.float32)
    average = jnp.mean(mixed, axis=-1, keepdims=True)
    centred = mixed - average
    variance = jnp.mean(centred * centred, axis=-1, keepdims=True)
    normed = (centred * lax.rsqrt(variance + 1e-05) * norm_gain).astype(jnp.bfloat16)
    inputs = normed
    preact = jnp.dot(
        inputs,
        lax.all_gather(proj_weight, "fsdp", axis=0, tiled=True),
        preferred_element_type=jnp.float32,
    )
    hidden = jax.nn.gelu(preact, approximate=True).astype(jnp.bfloat16)
    inputs = hidden
    branch = jnp.dot(
        inputs,
        lax.all_gather(out_weight, "fsdp", axis=0, tiled=True),
        preferred_element_type=jnp.float32,
    )
    return (mixed + branch).astype(jnp.bfloat16)[None]


def solution(mesh):
    placed = (
        P(("groups", "fsdp", "dp"), "sub", None),
        P(("groups", "dp"), "sub", None),
        P(("groups", "fsdp", "dp")),
        P(),
        P("fsdp", None),
        P("fsdp", None),
        P(None, "fsdp"),
    )
    return jax.shard_map(
        body,
        mesh=mesh,
        in_specs=placed,
        out_specs=P(("groups", "fsdp", "dp"), "sub", None),
        check_vma=False,
    )
```

profile of v0, /device:TPU:0, one launch (start us, length us, event | category | flops | bytes accessed | tf_op | source)
XLA Modules:
  0.0 289.0 jit_solution(17761163579044327469)
XLA Ops:
  6.5 0.0 copy-start
  6.5 0.0 all-gather.4.cloned.1.call-start
  6.5 1.5 copy-done
  8.1 2.5 convolution_convert_fusion
  10.6 0.0 all-gather.4.cloned.1.call-update
  10.6 0.0 all-gather.6.cloned.1.call-start
  10.7 0.7 all-gather.6.cloned.1.call-update
  11.4 0.0 all-gather.8.cloned.1.call-start
  11.4 0.7 all-gather.8.cloned.1.call-update
  12.7 1.6 copy.8
  14.3 46.6 %all-gather.4.cloned.1.call-done = bf16[2,384,1280]{1,2,0:T(8,128)(2,1)} async-done(((bf16[2,384,160]{1,2,0:T(8,128)(2,1)}), bf16[2,384,1280]{1,2,0:T(8,128)(2,1)}) %all-gather.4.cloned.1.call-update) | async-done | bytes 1966096 | tf_op jit(solution)/shard_map/all_gather | solution.py:12
  61.0 0.0 copy-start.1
  61.0 0.0 copy-start.2
  61.0 1.7 fusion.15
  62.7 0.1 copy-done.1
  62.8 0.4 multiply_reduce_fusion
  63.3 101.3 %all-gather.6.cloned.1.call-done = bf16[1280,2560]{1,0:T(8,128)(2,1)} async-done(((bf16[160,2560]{1,0:T(8,128)(2,1)}), bf16[1280,2560]{1,0:T(8,128)(2,1)}) %all-gather.6.cloned.1.call-update) | async-done | bytes 6553616 | tf_op jit(solution)/shard_map/all_gather | solution.py:22
  164.5 102.6 %all-gather.8.cloned.1.call-done = bf16[2560,1280]{1,0:T(8,128)(2,1)} async-done(((bf16[320,1280]{1,0:T(8,128)(2,1)}), bf16[2560,1280]{1,0:T(8,128)(2,1)}) %all-gather.8.cloned.1.call-update) | async-done | bytes 6553616 | tf_op jit(solution)/shard_map/all_gather | solution.py:29
  267.2 0.0 copy-done.2
  267.2 13.0 %fusion.9 = bf16[1,384,1280]{1,2,0:T(8,128)(2,1)} fusion(bf16[2560,1280]{1,0:T(8,128)(2,1)} %all-gather.8.cloned.1.call-done, bf16[1,384,1280]{1,2,0:T(8,128)(2,1)S(1)} %copy.8, bf16[1280,2560]{1,0:T(8,128)(2,1)} %all-gather.6.cloned.1.call-done, f32[1280]{0:T(1024)S(1)} %copy-done.2, f32[384]{0:T(512)S(1)} %add_rsqrt_fusion, ...), kind=kOutput, calls=%fused_computation.11 | convolution fusion | flops 5047910400 | bytes 18035712 | tf_op jit(solution)/shard_map/dot_general | solution.py:27
  280.2 2.2 copy.10
  (2 shorter events, 0.0 us)
Async XLA Ops:
  6.5 1.5 copy-start
  6.5 54.4 %all-gather.4.cloned.1.call-start = ((), (), s32[]{:S(2)}) async-start(), calls=%async_computation | async-start | bytes 2211840 | tf_op jit(solution)/shard_map/all_gather | solution.py:12
  10.6 153.9 %all-gather.6.cloned.1.call-start = ((), (), s32[]{:S(2)}) async-start(), calls=%async_computation.1 | async-start | bytes 7372800 | tf_op jit(solution)/shard_map/all_gather | solution.py:22
  11.4 255.8 %all-gather.8.cloned.1.call-start = ((), (), s32[]{:S(2)}) async-start(), calls=%async_computation.2 | async-start | bytes 7372800 | tf_op jit(solution)/shard_map/all_gather | solution.py:29
  61.0 1.8 copy-start.1
  61.0 206.2 %copy-start.2 = (f32[1280]{0:T(1024)S(1)}, f32[1280]{0:T(1024)}, u32[]{:S(2)}) copy-start(f32[1280]{0:T(1024)} %param.10) | copy-start | bytes 15364
Sparse Core Ops, SparseCore 0:
  10.7 50.2 all-gather.3
  63.2 101.3 all-gather.5
  166.7 100.3 all-gather.7
where the time goes:
time: 289 us
  waiting for transfers between devices  252 us (87%)
  matrix products  15.5 us (5%)
  between operations  13.8 us (5%)
  local copies, waits for them, and re-layouts  5.51 us (2%)
    all_gather x1, waiting for transfers between devices, body(): lax.all_gather(out_weight, 'fsdp', axis=0, tiled=True)  103 us
    all_gather x1, waiting for transfers between devices, body(): lax.all_gather(proj_weight, 'fsdp', axis=0, tiled=True)  101 us
    all_gather x1, waiting for transfers between devices, body(): gathered = lax.all_gather(columns, 'fsdp', axis=2, tiled=True)  46.6 us
    dot_general x1, matrix products, body(): jnp.dot(inputs, lax.all_gather(out_weight, 'fsdp', axis=0, tiled=True), p...  13 us
  transfers between devices with their start and end apart: 3, of which 3 were waited for; matrix products, arithmetic and copies ran while one was open for 1% of the time, Pallas kernels for 0%

commit v1 on v0

--- a/solution.py
+++ b/solution.py
@@ -9,7 +9,12 @@
     columns = jnp.einsum(
         "wpc,cd->wpd", golden, zero_weight, preferred_element_type=jnp.float32
     ).astype(jnp.bfloat16)
-    gathered = lax.all_gather(columns, "fsdp", axis=2, tiled=True)
+    ring = [columns]
+    for hop in range(7):
+        ring.append(lax.ppermute(ring[-1], "fsdp", [(dev, (dev + 1) % 8) for dev in range(8)]))
+    gathered = jnp.roll(
+        jnp.concatenate(ring[::-1], axis=2), (lax.axis_index("fsdp") + 1) * ring[0].shape[2], axis=2
+    )
     residual = lax.dynamic_index_in_dim(gathered, wafer_one, 0, keepdims=False)
     mixed = features[0].astype(jnp.float32) + residual.astype(jnp.float32)
     average = jnp.mean(mixed, axis=-1, keepdims=True)

time: 289 us -> 269 us (0.931)
  waiting for transfers between devices: 252 us -> 219 us
  local copies, waits for them, and re-layouts: 5.51 us -> 16.3 us
  starting transfers between devices: 0.08 us -> 3.05 us
    ppermute x0 -> x7, waiting for transfers between devices: none -> 96.8 us  [body(): lax.ppermute(ring[-1], 'fsdp', [(dev, (dev + 1) % 8) for dev in range(8)])]
    all_gather x1, waiting for transfers between devices: 101 us -> 16.3 us  [body(): lax.all_gather(proj_weight, 'fsdp', axis=0, tiled=True)]
    all_gather x1 -> x0, waiting for transfers between devices: 46.6 us -> none  [body(): gathered = lax.all_gather(columns, 'fsdp', axis=2, tiled=True)]
    unnamed x7 -> x38, local copies, waits for them, and re-layouts: 3.28 us -> 14 us
    ppermute x0 -> x7, starting transfers between devices: none -> 3.01 us  [body(): lax.ppermute(ring[-1], 'fsdp', [(dev, (dev + 1) % 8) for dev in range(8)])]
  transfers between devices with their start and end apart: 3 -> 9, of which waited for: 3 -> 9; matrix products, arithmetic and copies ran while one was open for 1% -> 5% of each run, Pallas kernels for 0% -> 0%
where the time goes in v1:
time: 269 us; the launch traced here: 268 us
  waiting for transfers between devices  219 us (81%)
  local copies, waits for them, and re-layouts  16.3 us (6%)
  matrix products  15 us (6%)
  between operations  14.3 us (5%)
  starting transfers between devices  3.05 us (1%)
    all_gather x1, waiting for transfers between devices, body(): lax.all_gather(out_weight, 'fsdp', axis=0, tiled=True)  104 us
    ppermute x7, waiting for transfers between devices, body(): lax.ppermute(ring[-1], 'fsdp', [(dev, (dev + 1) % 8) for dev in range(8)])  96.8 us
    all_gather x1, waiting for transfers between devices, body(): lax.all_gather(proj_weight, 'fsdp', axis=0, tiled=True)  16.3 us
    unnamed x38, local copies, waits for them, and re-layouts  14 us
    dot_general x1, matrix products, body(): jnp.dot(inputs, lax.all_gather(out_weight, 'fsdp', axis=0, tiled=True), p...  13.2 us
  transfers between devices with their start and end apart: 9, of which 9 were waited for; matrix products, arithmetic and copies ran while one was open for 5% of the time, Pallas kernels for 0%

profile of v1, /device:TPU:0, one launch (start us, length us, event | category | flops | bytes accessed | tf_op | source)
XLA Modules:
  0.0 268.1 jit_solution(14644195445013580783)
XLA Ops:
  6.5 0.0 copy-start
  6.5 0.0 all-gather.3.cloned.1.call-start
  6.5 0.7 all-gather.3.cloned.1.call-update
  7.3 0.0 all-gather.5.cloned.1.call-start
  7.3 0.7 all-gather.5.cloned.1.call-update
  8.0 0.1 copy-done
  8.1 1.8 convolution_convert_fusion
  9.9 3.0 %collective-permute-start = (bf16[2,384,160]{1,2,0:T(8,128)(2,1)S(1)}, bf16[2,384,160]{1,2,0:T(8,128)(2,1)S(1)}, u32[]{:S(2)}, u32[]{:S(2)}) collective-permute-start(bf16[2,384,160]{1,2,0:T(8,128)(2,1)S(1)} %convolution_convert_fusion), channel_id=1, source_target_pairs={{0,2},{2,4},{4,6},{6,8},{8,10},{10,12},{12,14},{14,0},{1,3},{3,5},... | collective-permute-start | bytes 737288 | tf_op jit(solution)/shard_map/ppermute | solution.py:14
  12.9 9.0 %collective-permute-done = bf16[2,384,160]{1,2,0:T(8,128)(2,1)S(1)} collective-permute-done((bf16[2,384,160]{1,2,0:T(8,128)(2,1)S(1)}, bf16[2,384,160]{1,2,0:T(8,128)(2,1)S(1)}, u32[]{:S(2)}, u32[]{:S(2)}) %collective-permute-start) | collective-permute-done | bytes 245792 | tf_op jit(solution)/shard_map/ppermute | solution.py:14
  21.9 0.0 collective-permute-start.1
  21.9 16.2 %collective-permute-done.1 = bf16[2,384,160]{1,2,0:T(8,128)(2,1)S(1)} collective-permute-done((bf16[2,384,160]{1,2,0:T(8,128)(2,1)S(1)}, bf16[2,384,160]{1,2,0:T(8,128)(2,1)S(1)}, u32[]{:S(2)}, u32[]{:S(2)}) %collective-permute-start.1) | collective-permute-done | bytes 245792 | tf_op jit(solution)/shard_map/ppermute | solution.py:14
  38.0 0.0 copy-start.2
  38.0 0.7 copy-done.2
  38.7 0.0 collective-permute-start.2
  38.7 15.9 %collective-permute-done.2 = bf16[2,384,160]{1,2,0:T(8,128)(2,1)S(1)} collective-permute-done((bf16[2,384,160]{1,2,0:T(8,128)(2,1)S(1)}, bf16[2,384,160]{1,2,0:T(8,128)(2,1)S(1)}, u32[]{:S(2)}, u32[]{:S(2)}) %collective-permute-start.2) | collective-permute-done | bytes 245792 | tf_op jit(solution)/shard_map/ppermute | solution.py:14
  54.7 0.0 copy-start.4
  54.7 0.7 copy-done.4
  55.4 0.0 collective-permute-start.3
  55.4 13.3 %collective-permute-done.3 = bf16[2,384,160]{1,2,0:T(8,128)(2,1)S(1)} collective-permute-done((bf16[2,384,160]{1,2,0:T(8,128)(2,1)S(1)}, bf16[2,384,160]{1,2,0:T(8,128)(2,1)S(1)}, u32[]{:S(2)}, u32[]{:S(2)}) %collective-permute-start.3) | collective-permute-done | bytes 245792 | tf_op jit(solution)/shard_map/ppermute | solution.py:14
  68.6 0.0 copy-start.6
  68.6 0.7 copy-done.6
  69.3 0.0 collective-permute-start.4
  69.3 14.9 %collective-permute-done.4 = bf16[2,384,160]{1,2,0:T(8,128)(2,1)S(1)} collective-permute-done((bf16[2,384,160]{1,2,0:T(8,128)(2,1)S(1)}, bf16[2,384,160]{1,2,0:T(8,128)(2,1)S(1)}, u32[]{:S(2)}, u32[]{:S(2)}) %collective-permute-start.4) | collective-permute-done | bytes 245792 | tf_op jit(solution)/shard_map/ppermute | solution.py:14
  84.3 0.0 copy-start.8
  84.3 0.7 copy-done.8
  85.0 0.0 collective-permute-start.5
  85.0 15.0 %collective-permute-done.5 = bf16[2,384,160]{1,2,0:T(8,128)(2,1)} collective-permute-done((bf16[2,384,160]{1,2,0:T(8,128)(2,1)S(1)}, bf16[2,384,160]{1,2,0:T(8,128)(2,1)}, u32[]{:S(2)}, u32[]{:S(2)}) %collective-permute-start.5) | collective-permute-done | bytes 245792 | tf_op jit(solution)/shard_map/ppermute | solution.py:14
  99.9 0.0 collective-permute-start.6
  100.6 1.6 copy.8
  102.2 0.0 copy-start.9
  102.2 0.0 copy-start.7
  102.2 0.0 copy-start.5
  102.2 0.0 copy-start.3
  102.2 12.6 %collective-permute-done.6 = bf16[2,384,160]{1,2,0:T(8,128)(2,1)} collective-permute-done((bf16[2,384,160]{1,2,0:T(8,128)(2,1)}, bf16[2,384,160]{1,2,0:T(8,128)(2,1)}, u32[]{:S(2)}, u32[]{:S(2)}) %collective-permute-start.6) | collective-permute-done | bytes 245792 | tf_op jit(solution)/shard_map/ppermute | solution.py:14
  114.8 1.0 constant_dynamic-update-slice_fusion.15
  115.8 1.0 constant_dynamic-update-slice_fusion.14
  116.7 1.0 constant_dynamic-update-slice_fusion.13
  117.7 1.0 constant_dynamic-update-slice_fusion.12
  118.7 1.0 constant_dynamic-update-slice_fusion.11
  119.7 1.0 constant_dynamic-update-slice_fusion.10
  120.8 0.0 copy-start.10
  120.8 1.0 constant_dynamic-update-slice_fusion.7
  121.8 1.0 constant_dynamic-update-slice_fusion.6
  122.8 0.0 copy-done.9
  122.8 0.0 copy-done.7
  122.9 0.0 copy-done.5
  123.0 0.0 copy-done.3
  123.1 0.0 copy-start.1
  123.1 0.4 fusion.15
  123.6 1.4 copy-done.1
  125.0 0.5 multiply_reduce_fusion
  125.5 16.3 %all-gather.3.cloned.1.call-done = bf16[1280,2560]{1,0:T(8,128)(2,1)} async-done(((bf16[160,2560]{1,0:T(8,128)(2,1)}), bf16[1280,2560]{1,0:T(8,128)(2,1)}) %all-gather.3.cloned.1.call-update) | async-done | bytes 6553616 | tf_op jit(solution)/shard_map/all_gather | solution.py:27
  141.8 104.0 %all-gather.5.cloned.1.call-done = bf16[2560,1280]{1,0:T(8,128)(2,1)} async-done(((bf16[320,1280]{1,0:T(8,128)(2,1)}), bf16[2560,1280]{1,0:T(8,128)(2,1)}) %all-gather.5.cloned.1.call-update) | async-done | bytes 6553616 | tf_op jit(solution)/shard_map/all_gather | solution.py:34
  245.8 0.0 copy-done.10
  245.8 13.2 %fusion.9 = bf16[1,384,1280]{1,2,0:T(8,128)(2,1)} fusion(bf16[2560,1280]{1,0:T(8,128)(2,1)} %all-gather.5.cloned.1.call-done, bf16[1,384,1280]{1,2,0:T(8,128)(2,1)S(1)} %copy.8, bf16[1280,2560]{1,0:T(8,128)(2,1)} %all-gather.3.cloned.1.call-done, f32[1280]{0:T(1024)S(1)} %copy-done.10, f32[384]{0:T(512)S(1)} %add_rsqrt_fusion, ...), kind=kOutput, calls=%fused_computation.11 | convolution fusion | flops 5047910400 | bytes 18036736 | tf_op jit(solution)/shard_map/dot_general | solution.py:32
  259.0 2.2 copy.10
  (10 shorter events, 0.3 us)
Async XLA Ops:
  6.5 1.5 copy-start
  6.5 135.3 %all-gather.3.cloned.1.call-start = ((), (), s32[]{:S(2)}) async-start(), calls=%async_computation | async-start | bytes 7372800 | tf_op jit(solution)/shard_map/all_gather | solution.py:27
  7.3 238.6 %all-gather.5.cloned.1.call-start = ((), (), s32[]{:S(2)}) async-start(), calls=%async_computation.1 | async-start | bytes 7372800 | tf_op jit(solution)/shard_map/all_gather | solution.py:34
  9.9 12.0 %collective-permute-start = (bf16[2,384,160]{1,2,0:T(8,128)(2,1)S(1)}, bf16[2,384,160]{1,2,0:T(8,128)(2,1)S(1)}, u32[]{:S(2)}, u32[]{:S(2)}) collective-permute-start(bf16[2,384,160]{1,2,0:T(8,128)(2,1)S(1)} %convolution_convert_fusion), channel_id=1, source_target_pairs={{0,2},{2,4},{4,6},{6,8},{8,10},{10,12},{12,14},{14,0},{1,3},{3,5},... | collective-permute-start | bytes 737288 | tf_op jit(solution)/shard_map/ppermute | solution.py:14
  21.9 16.2 %collective-permute-start.1 = (bf16[2,384,160]{1,2,0:T(8,128)(2,1)S(1)}, bf16[2,384,160]{1,2,0:T(8,128)(2,1)S(1)}, u32[]{:S(2)}, u32[]{:S(2)}) collective-permute-start(bf16[2,384,160]{1,2,0:T(8,128)(2,1)S(1)} %collective-permute-done), channel_id=1, source_target_pairs={{0,2},{2,4},{4,6},{6,8},{8,10},{10,12},{12,14},{14,0},{1,3},{3,5},... | collective-permute-start | bytes 737288 | tf_op jit(solution)/shard_map/ppermute | solution.py:14
  38.0 0.7 copy-start.2
  38.7 15.9 %collective-permute-start.2 = (bf16[2,384,160]{1,2,0:T(8,128)(2,1)S(1)}, bf16[2,384,160]{1,2,0:T(8,128)(2,1)S(1)}, u32[]{:S(2)}, u32[]{:S(2)}) collective-permute-start(bf16[2,384,160]{1,2,0:T(8,128)(2,1)S(1)} %collective-permute-done.1), channel_id=1, source_target_pairs={{0,2},{2,4},{4,6},{6,8},{8,10},{10,12},{12,14},{14,0},{1,3},{3,5},... | collective-permute-start | bytes 737288 | tf_op jit(solution)/shard_map/ppermute | solution.py:14
  54.7 0.7 copy-start.4
  55.4 13.3 %collective-permute-start.3 = (bf16[2,384,160]{1,2,0:T(8,128)(2,1)S(1)}, bf16[2,384,160]{1,2,0:T(8,128)(2,1)S(1)}, u32[]{:S(2)}, u32[]{:S(2)}) collective-permute-start(bf16[2,384,160]{1,2,0:T(8,128)(2,1)S(1)} %collective-permute-done.2), channel_id=1, source_target_pairs={{0,2},{2,4},{4,6},{6,8},{8,10},{10,12},{12,14},{14,0},{1,3},{3,5},... | collective-permute-start | bytes 737288 | tf_op jit(solution)/shard_map/ppermute | solution.py:14
  68.6 0.7 copy-start.6
  69.3 14.9 %collective-permute-start.4 = (bf16[2,384,160]{1,2,0:T(8,128)(2,1)S(1)}, bf16[2,384,160]{1,2,0:T(8,128)(2,1)S(1)}, u32[]{:S(2)}, u32[]{:S(2)}) collective-permute-start(bf16[2,384,160]{1,2,0:T(8,128)(2,1)S(1)} %collective-permute-done.3), channel_id=1, source_target_pairs={{0,2},{2,4},{4,6},{6,8},{8,10},{10,12},{12,14},{14,0},{1,3},{3,5},... | collective-permute-start | bytes 737288 | tf_op jit(solution)/shard_map/ppermute | solution.py:14
  84.3 0.7 copy-start.8
  85.0 15.0 %collective-permute-start.5 = (bf16[2,384,160]{1,2,0:T(8,128)(2,1)S(1)}, bf16[2,384,160]{1,2,0:T(8,128)(2,1)}, u32[]{:S(2)}, u32[]{:S(2)}) collective-permute-start(bf16[2,384,160]{1,2,0:T(8,128)(2,1)S(1)} %collective-permute-done.4), channel_id=1, source_target_pairs={{0,2},{2,4},{4,6},{6,8},{8,10},{10,12},{12,14},{14,0},{1,3},{3,5},... | collective-permute-start | bytes 737288 | tf_op jit(solution)/shard_map/ppermute | solution.py:14
  99.9 14.8 %collective-permute-start.6 = (bf16[2,384,160]{1,2,0:T(8,128)(2,1)}, bf16[2,384,160]{1,2,0:T(8,128)(2,1)}, u32[]{:S(2)}, u32[]{:S(2)}) collective-permute-start(bf16[2,384,160]{1,2,0:T(8,128)(2,1)} %collective-permute-done.5), channel_id=1, source_target_pairs={{0,2},{2,4},{4,6},{6,8},{8,10},{10,12},{12,14},{14,0},{1,3},{3,5},... | collective-permute-start | bytes 737288 | tf_op jit(solution)/shard_map/ppermute | solution.py:14
  102.2 20.6 %copy-start.9 = (bf16[2,384,160]{1,2,0:T(8,128)(2,1)S(1)}, bf16[2,384,160]{1,2,0:T(8,128)(2,1)}, u32[]{:S(2)}) copy-start(bf16[2,384,160]{1,2,0:T(8,128)(2,1)} %copy-done.8) | copy-start | bytes 737284
  102.2 20.7 %copy-start.7 = (bf16[2,384,160]{1,2,0:T(8,128)(2,1)S(1)}, bf16[2,384,160]{1,2,0:T(8,128)(2,1)}, u32[]{:S(2)}) copy-start(bf16[2,384,160]{1,2,0:T(8,128)(2,1)} %copy-done.6) | copy-start | bytes 737284
  102.2 20.7 %copy-start.5 = (bf16[2,384,160]{1,2,0:T(8,128)(2,1)S(1)}, bf16[2,384,160]{1,2,0:T(8,128)(2,1)}, u32[]{:S(2)}) copy-start(bf16[2,384,160]{1,2,0:T(8,128)(2,1)} %copy-done.4) | copy-start | bytes 737284
  102.2 20.8 %copy-start.3 = (bf16[2,384,160]{1,2,0:T(8,128)(2,1)S(1)}, bf16[2,384,160]{1,2,0:T(8,128)(2,1)}, u32[]{:S(2)}) copy-start(bf16[2,384,160]{1,2,0:T(8,128)(2,1)} %copy-done.2) | copy-start | bytes 737284
  120.8 125.0 %copy-start.10 = (f32[1280]{0:T(1024)S(1)}, f32[1280]{0:T(1024)}, u32[]{:S(2)}) copy-start(f32[1280]{0:T(1024)} %param.10) | copy-start | bytes 15364
  123.1 1.9 copy-start.1
Sparse Core Ops, SparseCore 0:
  9.5 132.2 all-gather.2
  144.0 101.7 all-gather.4
